TPU v7x, 32 devices: a whole 2x2x4 slice. The times are simulated.
32 devices in a mesh: pb: 4 (over z), ka: 4 (over y, core), ha: 2 (over x).
Axes of the slice: x: 2, y: 2, z: 4, core: 2. Of those that a mesh axis runs over, the one named last changes fastest.
Arguments:
- queries: bfloat16 [4096, 4096], P('pb', 'ha'), may hold values from -512 to 512
- keys: bfloat16 [8, 4, 128, 512], P('pb', 'ka', None, 'ha'), may hold values from -6 to 6
- values: bfloat16 [8, 4, 128, 512], P('pb', 'ka', None, 'ha'), may hold values from -6 to 6
- q_order: int32 [32], P('pb'), may hold values from 0 to 31, as said below
- block_mask: int32 [32, 32], P('pb'), may hold values from 0 to 1, as said below
Outputs:
- attended: bfloat16 [4096, 4096], P(('pb', 'ka'), 'ha')
Inputs may be any that keep to these rules, and one draw needn't show every extreme that they name: `q_order`: slots 2m and 2m+1 hold query blocks i and 31 - i for some i, in either order; every block sits in exactly one slot. block_mask[s, b] is 1 only where b <= q_order[s], and block_mask[s, q_order[s]] is 1. For every m and every r below 4, slots 2m and 2m+1 together list at most 4 key blocks b with b % 4 == r, and exactly 4 for some m and r in every draw.
All inputs are finite; a program needn't handle non-finite values.
Results may differ from a plain program's by a relative error of at most 0.0042.
Values may be sent and summed in bfloat16 or wider, within the bound.
No kernel may reach another device: no remote copies, remote signals or barrier semaphores. Data moves between devices by JAX's collectives and lax.ppermute only.
A program may use at most 128 MiB of HBM per device.

v0:
```python
import functools
import math

import jax
import jax.numpy as jnp
from jax import lax
from jax.experimental import pallas as pl
from jax.experimental.pallas import tpu as pltpu
from jax.sharding import PartitionSpec as P

HEAD_DIM = 128
MASKED = -1e30
HIDDEN = -1e38
HEADROOM = 64.0
PARTS = 8
LIMIT = 10
SMALL = 4
STAGES = 4


def folded(size):
    return list(range(0, size, 2)) + list(range(1, size, 2))[::-1]


def along_ring(array, size, step=1):
    ring = folded(size)
    return lax.ppermute(array, "pb", [(ring[i], ring[(i + step) % size]) for i in range(size)])


def ring_source(at, size, hops):
    place = jnp.where(at % 2 == 0, at // 2, size - 1 - at // 2)
    place = lax.rem(place + (size - hops), size)
    return jnp.where(place < (size + 1) // 2, 2 * place, 2 * (size - 1 - place) + 1)


def turn(array, size, cores, ring_step, core_step):
    rings = size // cores
    pairs = []
    for ring in range(rings):
        for core in range(cores):
            to = ((ring + ring_step) % rings) * cores + (core + core_step) % cores
            pairs.append((ring * cores + core, to))
    return lax.ppermute(array, "ka", pairs)


def dot(a, b, b_dim):
    return lax.dot_general(a, b, (((1,), (b_dim,)), ((), ())), preferred_element_type=jnp.float32)


def copy_rows(source, target, sems):
    step = source.shape[0] // PARTS
    copies = [
        pltpu.make_async_copy(
            source.at[pl.ds(i * step, step)], target.at[pl.ds(i * step, step)], sems.at[i]
        )
        for i in range(PARTS)
    ]
    for copy in copies:
        copy.start()
    return copies


def attend_stage(plan, first, last, ahead, table_ref, q_ref, *refs):
    pb, ka, cores, class_local, places, earlier, slots, turned = plan
    count = len(places)
    pieces, refs = refs[:count], refs[count:]
    old_pieces, refs = refs[:ahead], refs[ahead:]
    if not first:
        refs = refs[1:]
    acc, refs = refs[0], refs[1:]
    if last:
        out_ref, refs = refs[0], refs[1:]
    k_pool, v_pool, held_weights, entries, units, refs = *refs[:5], refs[5:]
    rows = acc.shape[1]
    block_rows = q_ref.shape[0] // slots
    group = rows // block_rows
    rings = ka // cores
    own_slots = slots // cores
    p_at, k_at = lax.axis_index("pb"), lax.axis_index("ka")
    ring_at, core_at = k_at // cores, lax.rem(k_at, cores)
    scale = math.log2(math.e) / math.sqrt(HEAD_DIM)

    def ids(where):
        found = []
        for hops, y, offsets in where:
            ring = lax.rem(ring_at + (rings - y), rings)
            for z in hops:
                source = ring_source(p_at, pb, z)
                for c in offsets:
                    core = lax.rem(core_at + (cores - c), cores)
                    for t in range(class_local):
                        found.append((source * class_local + t) * ka + ring * cores + core)
        return found

    def pool_from(refs_in, at, k_out, v_out):
        for piece in refs_in:
            for i in range(0, piece.shape[0], 2 * class_local):
                span = slice(at, at + class_local)
                k_out[span] = piece[i : i + class_local]
                value = piece[i + class_local : i + 2 * class_local]
                v_out[span, :, :HEAD_DIM] = value
                v_out[span, :, HEAD_DIM:] = jnp.ones(value.shape, v_out.dtype)
                at += class_local

    nothing = sum(piece.shape[0] for piece in pieces) // 2

    if last:
        mine = lax.rem(core_at + turned, cores) * own_slots
        slot_ids = [mine + i for i in range(own_slots)]
    else:
        slot_ids = list(range(slots))

    row_id = lax.broadcasted_iota(jnp.int32, (block_rows, block_rows), 0)
    col_id = lax.broadcasted_iota(jnp.int32, (block_rows, block_rows), 1)
    pool_from(pieces, 0, k_pool, v_pool)
    k_pool[nothing] = jnp.zeros(k_pool.shape[1:], k_pool.dtype)
    v_pool[nothing] = jnp.zeros(v_pool.shape[1:], v_pool.dtype)

    blocks = ids(places)
    unit_count = jnp.int32(0)
    for s in slot_ids:
        row = ring_at * slots + s
        own = table_ref[row, 0]
        place = 2 * unit_count
        for index, block in enumerate(blocks):
            entries[place] = jnp.where(block == own, index + nothing + 1, index)
            place = place + table_ref[row, 1 + block]
        entries[place] = nothing
        ends = lax.div(place + 1, 2)
        if first:

            @pl.when(ends == unit_count)
            def _(s=s):
                acc[s] = jnp.zeros(acc.shape[1:], acc.dtype)


        def mark(u, carry, s=s):
            units[u] = s
            return carry

        lax.fori_loop(unit_count, ends, mark, 0)
        unit_count = ends
    def query_rows(s):
        return jnp.concatenate(
            [
                q_ref[
                    pl.ds(pl.multiple_of(s * block_rows, block_rows), block_rows),
                    x * HEAD_DIM : (x + 1) * HEAD_DIM,
                ]
                for x in range(group)
            ],
            axis=0,
        )

    def pair_of(u):
        raw = [entries[2 * u], entries[2 * u + 1]]
        owns = [entry > nothing for entry in raw]
        return owns, [jnp.where(o, e - (nothing + 1), e) for o, e in zip(owns, raw)]

    def weigh(u):
        owns, index = pair_of(u)
        keys = jnp.concatenate([k_pool[i] for i in index], axis=0)
        reach = jnp.concatenate(
            [
                jnp.where(col_id <= row_id + jnp.where(own, 0, block_rows), 0.0, HIDDEN)
                for own in owns
            ],
            axis=1,
        )
        power = dot(query_rows(units[u]), keys, 1) * scale
        power = power + jnp.concatenate([reach] * group, axis=0)
        held_weights[...] = jnp.exp2(power).astype(held_weights.dtype)

    def add(u):
        _, index = pair_of(u)
        s = units[u]
        values = jnp.concatenate([v_pool[i] for i in index], axis=0)
        added = dot(held_weights[...], values, 0)
        old = acc[s]
        if first:
            fresh = (u == 0) | (units[jnp.maximum(u - 1, 0)] != s)
            old = jnp.where(fresh, 0.0, old)
        acc[s] = old + added

    @pl.when(unit_count > 0)
    def _():
        weigh(0)

        def both(u, carry):
            add(u)
            weigh(u + 1)
            return carry

        lax.fori_loop(0, unit_count - 1, both, 0)
        add(unit_count - 1)

    if not last:
        return

    top, k_all, v_all = refs

    def finish(s, i):
        under = acc[s, :, HEAD_DIM:]
        result = (acc[s, :, :HEAD_DIM] / under).astype(out_ref.dtype)
        for x in range(group):
            out_ref[
                i * block_rows : (i + 1) * block_rows, x * HEAD_DIM : (x + 1) * HEAD_DIM
            ] = result[x * block_rows : (x + 1) * block_rows]
        low = high = [under[j : j + 8] for j in range(0, rows, 8)]
        while len(low) > 1:
            low = [functools.reduce(jnp.minimum, low[j : j + 2]) for j in range(0, len(low), 2)]
            high = [functools.reduce(jnp.maximum, high[j : j + 2]) for j in range(0, len(high), 2)]
        return low[0], high[0]

    low, high = zip(*[finish(s, i) for i, s in enumerate(slot_ids)])
    low, high = functools.reduce(jnp.minimum, low), functools.reduce(jnp.maximum, high)
    safe = (low > 2.0**-HEADROOM) & (high < 2.0**HEADROOM)

    @pl.when(jnp.min(jnp.where(safe, 1.0, 0.0)) < 0.5)
    def _():
        pool_from(old_pieces, 0, k_all, v_all)
        pool_from(pieces, sum(p.shape[0] for p in old_pieces) // 2, k_all, v_all)
        blocks_all = ids(earlier) + blocks
        for i, s in enumerate(slot_ids):
            row = ring_at * slots + s
            own = table_ref[row, 0]
            place = jnp.int32(0)
            for index, block in enumerate(blocks_all):
                entries[place] = jnp.where(block == own, index + len(blocks_all), index)
                place = place + table_ref[row, 1 + block]
            acc[s] = jnp.zeros(acc.shape[1:], acc.dtype)
            top[...] = jnp.full(top.shape, MASKED, top.dtype)

            def one_block(e, carry, s=s):
                is_own = entries[e] >= len(blocks_all)
                index = jnp.where(is_own, entries[e] - len(blocks_all), entries[e])
                reach = jnp.where(
                    col_id <= row_id + jnp.where(is_own, 0, block_rows), 0.0, HIDDEN
                )
                scores = dot(query_rows(s), k_all[index], 1)
                weights, shrinks = [], []
                for x in range(group):
                    span = slice(x * block_rows, (x + 1) * block_rows)
                    power = scores[span] * scale + reach
                    new = jnp.maximum(top[span], jnp.max(power, axis=1, keepdims=True))
                    shrink = jnp.exp2(top[span] - new)
                    top[span] = new
                    weights.append(jnp.exp2(power - new).astype(jnp.bfloat16))
                    shrinks.append(jnp.concatenate([shrink, shrink], axis=1))
                added = dot(jnp.concatenate(weights, axis=0), v_all[index], 0)
                acc[s] = acc[s] * jnp.concatenate(shrinks, axis=0) + added
                return carry

            lax.fori_loop(0, place, one_block, 0)
            finish(s, i)


def cut(cores, *refs):
    ins, out_ref = refs[:-1], refs[-1]
    count = ins[0].shape[0]
    width = out_ref.shape[2]
    core = lax.rem(lax.axis_index("ka"), cores)
    for c in range(cores):

        @pl.when(core == c)
        def _():
            for i, ref in enumerate(ins):
                out_ref[i * count : (i + 1) * count] = ref[
                    :, 0, :, c * width : (c + 1) * width
                ]


def fetch(cores, queries_ref, out_ref, sems):
    rows, width = out_ref.shape
    at = lax.axis_index("ka")
    copies = copy_rows(
        queries_ref.at[
            pl.ds(pl.multiple_of(at // cores * rows, HEAD_DIM), rows),
            pl.ds(pl.multiple_of(lax.rem(at, cores) * width, HEAD_DIM), width),
        ],
        out_ref,
        sems,
    )
    for copy in copies:
        copy.wait()


def join(cores, own_ref, other_ref, out_ref, sems):
    width = own_ref.shape[1]
    core = lax.rem(lax.axis_index("ka"), cores)
    copies = []
    for i, ref in enumerate((own_ref, other_ref)):
        at = pl.multiple_of(lax.rem(core + (cores - i), cores) * width, HEAD_DIM)
        copies += copy_rows(ref, out_ref.at[:, pl.ds(at, width)], sems.at[i])
    for copy in copies:
        copy.wait()


def on_device(queries, keys, values, q_order, block_mask):
    pb, ka = lax.axis_size("pb"), lax.axis_size("ka")
    class_local, _, block_rows, kv_width = keys.shape
    cores = 2 if ka % 2 == 0 and kv_width == 2 * HEAD_DIM else 1
    rings = ka // cores
    head_width = kv_width // cores
    width = queries.shape[1] // cores
    rows = width // head_width * block_rows
    own_slots = queries.shape[0] // block_rows // ka
    slots = own_slots * cores

    vmem = pl.BlockSpec(memory_space=pltpu.VMEM)
    smem = pl.BlockSpec(memory_space=pltpu.SMEM)

    anywhere = pl.BlockSpec(memory_space=pl.ANY)
    stages = min(STAGES, pb)
    sources = pb // stages

    own_queries = pl.pallas_call(
        functools.partial(fetch, cores),
        out_shape=jax.ShapeDtypeStruct((slots * block_rows, width), queries.dtype),
        in_specs=[anywhere],
        out_specs=vmem,
        scratch_shapes=[pltpu.SemaphoreType.DMA((PARTS,))],
        compiler_params=pltpu.CompilerParams(vmem_limit_bytes=50 * 2**20),
    )(queries)
    raw = [keys, values]
    for c in range(1, cores):
        raw += [turn(keys, ka, cores, 0, c), turn(values, ka, cores, 0, c)]
    start = pl.pallas_call(
        functools.partial(cut, cores),
        out_shape=jax.ShapeDtypeStruct(
            (2 * cores * class_local, block_rows, head_width), keys.dtype
        ),
        in_specs=[vmem] * len(raw),
        out_specs=vmem,
        compiler_params=pltpu.CompilerParams(vmem_limit_bytes=SMALL * 2**20),
    )(*raw)

    start, q_order = lax.optimization_barrier((start, q_order))
    table = jnp.concatenate([q_order[:, None], block_mask], axis=1)
    def blocks_of(where):
        return sum(len(hops) * len(offsets) * class_local for hops, _, offsets in where)

    def call(first, last, turned, pieces, places, earlier, own_queries, state, extra):
        held = blocks_of(places)
        everything = held + blocks_of(earlier)
        here = own_slots if last else slots
        outs = [jax.ShapeDtypeStruct((slots, rows, 2 * HEAD_DIM), jnp.float32)]
        scratch = [
            pltpu.VMEM((held + 1, block_rows, HEAD_DIM), jnp.bfloat16),
            pltpu.VMEM((held + 1, block_rows, 2 * HEAD_DIM), jnp.bfloat16),
            pltpu.VMEM((rows, 2 * block_rows), jnp.bfloat16),
            pltpu.SMEM((max(here * (held + 1) + 1, everything + 1),), jnp.int32),
            pltpu.SMEM((here * (held // 2 + 1),), jnp.int32),
        ]
        if last:
            outs.append(jax.ShapeDtypeStruct((own_slots * block_rows, width), queries.dtype))
            scratch += [
                pltpu.VMEM((rows, HEAD_DIM), jnp.float32),
                pltpu.VMEM((everything, block_rows, HEAD_DIM), jnp.bfloat16),
                pltpu.VMEM((everything, block_rows, 2 * HEAD_DIM), jnp.bfloat16),
            ]
        pooled = held + (everything if last else 0)
        room = LIMIT * 2**20 + pooled * block_rows * HEAD_DIM * 6
        state_at = 2 + len(places) + len(extra)
        return pl.pallas_call(
            functools.partial(
                attend_stage,
                (pb, ka, cores, class_local, places, earlier, slots, turned),
                first,
                last,
                len(extra),
            ),
            out_shape=outs,
            in_specs=[smem]
            + [vmem] * (1 + len(places))
            + [vmem] * (len(extra) + len(state)),
            out_specs=[vmem] * len(outs),
            input_output_aliases={state_at + i: i for i in range(len(state))},
            scratch_shapes=scratch,
            compiler_params=pltpu.CompilerParams(vmem_limit_bytes=room),
            cost_estimate=pl.CostEstimate(
                flops=2**31, bytes_accessed=2**22, transcendentals=2**20
            ),
        )(table, own_queries, *pieces, *extra, *state)

    def along(array, count):
        found = []
        for _ in range(count):
            array = along_ring(array, pb)
            found.append(array)
        return found

    def stacked(arrays):
        return arrays[0] if len(arrays) == 1 else jnp.concatenate(arrays, axis=0)

    def beside(array):
        found = []
        for _ in range(rings - 1):
            array = turn(array, ka, cores, 1, 0)
            found.append(array)
        return found

    every = list(range(cores))
    state, earlier, before = [], [], []

    def work(state, pieces, places):
        state = call(not earlier, False, 0, pieces, places, earlier, own_queries, state, [])
        earlier.extend(places)
        before.extend(pieces)
        return state

    if rings == cores == 2 and pb == STAGES:
        tie = lax.optimization_barrier
        half = start.shape[0] // 2
        on = along_ring(start, pb)
        later, table = tie((start, table))
        others = beside(later)[0]
        state = work(state, [start], [([0], 0, every)])
        again, state = tie((start, state))
        back = along_ring(again, pb, -1)
        on, state = tie((on, state))
        on_others = beside(on)[0]
        state = work(state, [on], [([1], 0, every)])
        on, back, state = tie((on, back, state))
        back_others, two = beside(back)[0], along_ring(on, pb)
        state = work(state, [back, others], [([pb - 1], 0, every), ([0], 1, every)])
        on_others, state = tie((on_others, state))
        two_high = along_ring(on_others[half:], pb)
        state = work(state, [on_others], [([1], 1, every)])
        two, state = tie((two, state))
        two_low = turn(two[:half], ka, cores, 1, 0)
        state = work(state, [two], [([2], 0, every)])
        state = work(state, [back_others], [([pb - 1], 1, every)])
        pieces, places = [two_low, two_high], [([2], 1, [0]), ([2], 1, [1])]
    else:
        arrived = [start] + along(start, sources - 1)
        others, places = [], []
        for stage in range(stages):
            hops = range(stage * sources, (stage + 1) * sources)
            if stage:
                arrived, others, state = lax.optimization_barrier((arrived, others, state))
            near = stacked(arrived)
            pieces, places = [near] + others, [(hops, 0, every)] + places
            if stage < stages - 1:
                arrived = along(arrived[-1], sources)
            others = beside(near)
            state = work(state, pieces, places)
            places = [(hops, y, every) for y in range(1, rings)]
        pieces = others
    halves = []
    for c in reversed(range(cores)):
        *state, half = call(False, True, c, pieces, places, earlier, own_queries, state, before)
        halves.append(half)
    if cores == 1:
        return halves[0]
    return pl.pallas_call(
        functools.partial(join, cores),
        out_shape=jax.ShapeDtypeStruct((own_slots * block_rows, cores * width), queries.dtype),
        in_specs=[vmem] * 2,
        out_specs=anywhere,
        scratch_shapes=[pltpu.SemaphoreType.DMA((cores, PARTS))],
        compiler_params=pltpu.CompilerParams(vmem_limit_bytes=SMALL * 2**20),
    )(halves[1], turn(halves[0], ka, cores, 0, 1))


def solution(mesh):
    in_specs = (
        P("pb", "ha"),
        P("pb", "ka", None, "ha"),
        P("pb", "ka", None, "ha"),
        P("pb"),
        P("pb", None),
    )
    out_specs = P(("pb", "ka"), "ha")
    return jax.shard_map(
        on_device, mesh=mesh, in_specs=in_specs, out_specs=out_specs, check_vma=False
    )
```

profile of v0, /device:TPU:28, one launch (start us, length us, event | category | flops | bytes accessed | tf_op | source)
XLA Modules:
  0.0 58.0 jit_solution(12752183450091427)
XLA Ops:
  0.0 0.0 copy-start
  0.0 0.0 copy-start.1
  0.0 0.0 copy-start.3
  0.0 0.0 copy-start.2
  0.0 0.1 collective-permute-start
  0.1 0.5 collective-permute-start.1
  0.6 1.3 %shard_map.56.q_ref = bf16[512,1024]{1,0:T(8,128)(2,1)S(1)} custom-call(bf16[1024,2048]{1,0:T(8,128)(2,1)} %queries_ref.1), custom_call_target="tpu_custom_call" | custom-call | tf_op jit(solution)/shard_map/pallas_call | solution.py:317
  2.0 0.0 collective-permute-done.refs_2_
  2.0 0.0 collective-permute-done.1.refs_3_
  2.0 0.0 copy-done
  2.0 0.0 copy-done.1
  2.0 0.1 shard_map.55.refs_0_.refs_2_
  2.1 0.0 copy-done.3
  2.1 0.1 copy.13
  2.2 0.3 collective-permute-start.2
  2.5 0.0 copy-done.2
  2.5 0.1 pad_add_fusion.table_ref
  2.6 1.0 %shard_map.57.refs_1_ = f32[4,1024,256]{2,1,0:T(8,128)S(1)} custom-call(s32[8,33]{1,0:T(8,128)S(1)} %pad_add_fusion.table_ref, bf16[512,1024]{1,0:T(8,128)(2,1)S(1)} %shard_map.56.q_ref, bf16[8,128,128]{2,1,0:T(8,128)(2,1)S(1)} %shard_map.55.refs_0_.refs_2_), custom_call_target="tpu_custom_call" | custom-call | flops 2147483648 | bytes 4194304 | tf_op jit(solution)/shard_map/pallas_call | solution.py:365
  3.6 2.7 %collective-permute-start.3 = (bf16[8,128,128]{2,1,0:T(8,128)(2,1)S(1)}, bf16[8,128,128]{2,1,0:T(8,128)(2,1)S(1)}, u32[]{:S(2)}, u32[]{:S(2)}) collective-permute-start(bf16[8,128,128]{2,1,0:T(8,128)(2,1)S(1)} %shard_map.55.refs_0_.refs_2_), channel_id=1, source_target_pairs={{0,8},{16,0},{24,16},{8,24},{1,9},{17,1},{25,17},{9,25},{2,10},{18... | collective-permute-start | bytes 786440 | tf_op jit(solution)/shard_map/ppermute | solution.py:27
  6.3 0.5 collective-permute-start.6
  6.8 3.8 %collective-permute-done.2.refs_0_.refs_3_ = bf16[8,128,128]{2,1,0:T(8,128)(2,1)S(1)} collective-permute-done((bf16[8,128,128]{2,1,0:T(8,128)(2,1)S(1)}, bf16[8,128,128]{2,1,0:T(8,128)(2,1)S(1)}, u32[]{:S(2)}, u32[]{:S(2)}) %collective-permute-start.2) | collective-permute-done | bytes 262176 | tf_op jit(solution)/shard_map/ppermute | solution.py:27
  10.6 0.5 collective-permute-start.5
  11.1 1.8 %shard_map.58.refs_2_ = f32[4,1024,256]{2,1,0:T(8,128)S(1)} custom-call(s32[8,33]{1,0:T(8,128)S(1)} %pad_add_fusion.table_ref, bf16[512,1024]{1,0:T(8,128)(2,1)S(1)} %shard_map.56.q_ref, bf16[8,128,128]{2,1,0:T(8,128)(2,1)S(1)} %collective-permute-done.2.refs_0_.refs_3_, f32[4,1024,256]{2,1,0:T(8,128)S(1)} %shard_map.57.refs_1_), custom_call_target="tpu_custom_call", output_to_operand_aliasing={{}: (3, {})} | custom-call | flops 2147483648 | bytes 4194304 | tf_op jit(solution)/shard_map/pallas_call | solution.py:365
  13.0 4.0 %collective-permute-done.3.refs_0_.refs_4_ = bf16[8,128,128]{2,1,0:T(8,128)(2,1)S(1)} collective-permute-done((bf16[8,128,128]{2,1,0:T(8,128)(2,1)S(1)}, bf16[8,128,128]{2,1,0:T(8,128)(2,1)S(1)}, u32[]{:S(2)}, u32[]{:S(2)}) %collective-permute-start.3) | collective-permute-done | bytes 262176 | tf_op jit(solution)/shard_map/ppermute | solution.py:27
  16.9 0.6 %collective-permute-start.4 = (bf16[8,128,128]{2,1,0:T(8,128)(2,1)S(1)}, bf16[8,128,128]{2,1,0:T(8,128)(2,1)S(1)}, u32[]{:S(2)}, u32[]{:S(2)}) collective-permute-start(bf16[8,128,128]{2,1,0:T(8,128)(2,1)S(1)} %collective-permute-done.2.refs_0_.refs_3_), channel_id=1, source_target_pairs={{0,16},{16,24},{24,8},{8,0},{1,17},{17,25},{25,9},{9,1},{2,18},{18... | collective-permute-start | bytes 786440 | tf_op jit(solution)/shard_map/ppermute | solution.py:27
  17.5 0.5 collective-permute-start.9
  18.0 0.0 collective-permute-done.6.refs_1_.refs_5_
  18.0 1.9 %shard_map.59.refs_1_ = f32[4,1024,256]{2,1,0:T(8,128)S(1)} custom-call(s32[8,33]{1,0:T(8,128)S(1)} %pad_add_fusion.table_ref, bf16[512,1024]{1,0:T(8,128)(2,1)S(1)} %shard_map.56.q_ref, bf16[8,128,128]{2,1,0:T(8,128)(2,1)S(1)} %collective-permute-done.3.refs_0_.refs_4_, ...), custom_call_target="tpu_custom_call", output_to_operand_aliasing={{}: (4, {})} | custom-call | flops 2147483648 | bytes 4194304 | tf_op jit(solution)/shard_map/pallas_call | solution.py:365
  20.0 0.0 collective-permute-done.5.refs_0_.refs_6_
  20.0 1.8 %shard_map.60.refs_1_ = f32[4,1024,256]{2,1,0:T(8,128)S(1)} custom-call(s32[8,33]{1,0:T(8,128)S(1)} %pad_add_fusion.table_ref, bf16[512,1024]{1,0:T(8,128)(2,1)S(1)} %shard_map.56.q_ref, bf16[8,128,128]{2,1,0:T(8,128)(2,1)S(1)} %collective-permute-done.5.refs_0_.refs_6_, f32[4,1024,256]{2,1,0:T(8,128)S(1)} %shard_map.59.refs_1_), custom_call_target="tpu_custom_call", output_to_operand_aliasing={{}: (3, {})} | custom-call | flops 2147483648 | bytes 4194304 | tf_op jit(solution)/shard_map/pallas_call | solution.py:365
  21.8 3.3 %collective-permute-done.4.refs_0_.refs_7_ = bf16[8,128,128]{2,1,0:T(8,128)(2,1)S(1)} collective-permute-done((bf16[8,128,128]{2,1,0:T(8,128)(2,1)S(1)}, bf16[8,128,128]{2,1,0:T(8,128)(2,1)S(1)}, u32[]{:S(2)}, u32[]{:S(2)}) %collective-permute-start.4) | collective-permute-done | bytes 262176 | tf_op jit(solution)/shard_map/ppermute | solution.py:27
  25.2 1.2 %collective-permute-start.8 = (bf16[4,128,128]{2,1,0:T(8,128)(2,1)S(1)}, bf16[4,128,128]{2,1,0:T(8,128)(2,1)S(1)}, u32[]{:S(2)}, u32[]{:S(2)}) collective-permute-start(bf16[4,128,128]{2,1,0:T(8,128)(2,1)S(1)} %slice.7), channel_id=1, source_target_pairs={{0,16},{16,24},{24,8},{8,0},{1,17},{17,25},{25,9},{9,1},{2,18},{18... | collective-permute-start | bytes 393224 | tf_op jit(solution)/shard_map/ppermute | solution.py:27
  26.4 1.0 %collective-permute-start.7 = (bf16[4,128,128]{2,1,0:T(8,128)(2,1)S(1)}, bf16[4,128,128]{2,1,0:T(8,128)(2,1)S(1)}, u32[]{:S(2)}, u32[]{:S(2)}) collective-permute-start(bf16[4,128,128]{2,1,0:T(8,128)(2,1)S(1)} %slice.6), channel_id=1, source_target_pairs={{0,4},{2,6},{4,0},{6,2},{1,5},{3,7},{5,1},{7,3},{8,12},{10,14},{12... | collective-permute-start | bytes 393224 | tf_op jit(solution)/shard_map/ppermute | solution.py:43
  27.4 2.7 %shard_map.61.refs_1_ = f32[4,1024,256]{2,1,0:T(8,128)S(1)} custom-call(s32[8,33]{1,0:T(8,128)S(1)} %pad_add_fusion.table_ref, bf16[512,1024]{1,0:T(8,128)(2,1)S(1)} %shard_map.56.q_ref, bf16[8,128,128]{2,1,0:T(8,128)(2,1)S(1)} %collective-permute-done.4.refs_0_.refs_7_, f32[4,1024,256]{2,1,0:T(8,128)S(1)} %shard_map.60.refs_1_), custom_call_target="tpu_custom_call", output_to_operand_aliasing={{}: (3, {})} | custom-call | flops 2147483648 | bytes 4194304 | tf_op jit(solution)/shard_map/pallas_call | solution.py:365
  30.2 0.0 collective-permute-done.9.refs_0_.refs_8_
  30.2 2.3 %shard_map.62.refs_9_ = f32[4,1024,256]{2,1,0:T(8,128)S(1)} custom-call(s32[8,33]{1,0:T(8,128)S(1)} %pad_add_fusion.table_ref, bf16[512,1024]{1,0:T(8,128)(2,1)S(1)} %shard_map.56.q_ref, bf16[8,128,128]{2,1,0:T(8,128)(2,1)S(1)} %collective-permute-done.9.refs_0_.refs_8_, f32[4,1024,256]{2,1,0:T(8,128)S(1)} %shard_map.61.refs_1_), custom_call_target="tpu_custom_call", output_to_operand_aliasing={{}: (3, {})} | custom-call | flops 2147483648 | bytes 4194304 | tf_op jit(solution)/shard_map/pallas_call | solution.py:365
  32.4 0.0 collective-permute-done.8.refs_1_
  32.4 0.0 collective-permute-done.7.refs_0_
  32.5 2.2 %shard_map.63 = (f32[4,1024,256]{2,1,0:T(8,128)S(1)}, bf16[256,1024]{1,0:T(8,128)(2,1)S(1)}) custom-call(s32[8,33]{1,0:T(8,128)S(1)} %pad_add_fusion.table_ref, bf16[512,1024]{1,0:T(8,128)(2,1)S(1)} %shard_map.56.q_ref, bf16[4,128,128]{2,1,0:T(8,128)(2,1)S(1)} %collective-permute-done.7.refs_0_, ...), custom_call_target="tpu_custom_call", output_to_operand_aliasing={{0}: (11, {})} | custom-call | flops 2147483648 | bytes 4194304 | tf_op jit(solution)/shard_map/pallas_call | solution.py:365
  34.7 9.5 %collective-permute-start.10 = (bf16[256,1024]{1,0:T(8,128)(2,1)S(1)}, bf16[256,1024]{1,0:T(8,128)(2,1)S(1)}, u32[]{:S(2)}, u32[]{:S(2)}) collective-permute-start(bf16[256,1024]{1,0:T(8,128)(2,1)S(1)} %get-tuple-element.40), channel_id=1, source_target_pairs={{0,2},{2,0},{4,6},{6,4},{1,3},{3,1},{5,7},{7,5},{8,10},{10,8},{12,... | collective-permute-start | bytes 1572872 | tf_op jit(solution)/shard_map/ppermute | solution.py:43
  44.2 12.7 %shard_map.64 = (f32[4,1024,256]{2,1,0:T(8,128)S(1)}, bf16[256,1024]{1,0:T(8,128)(2,1)S(1)}) custom-call(s32[8,33]{1,0:T(8,128)S(1)} %pad_add_fusion.table_ref, bf16[512,1024]{1,0:T(8,128)(2,1)S(1)} %shard_map.56.q_ref, bf16[4,128,128]{2,1,0:T(8,128)(2,1)S(1)} %collective-permute-done.7.refs_0_, ...), custom_call_target="tpu_custom_call", output_to_operand_aliasing={{0}: (11, {})} | custom-call | flops 2147483648 | bytes 4194304 | tf_op jit(solution)/shard_map/pallas_call | solution.py:365
  56.9 0.0 collective-permute-done.10.other_ref
  56.9 1.1 %shard_map.65 = bf16[256,2048]{1,0:T(8,128)(2,1)} custom-call(bf16[256,1024]{1,0:T(8,128)(2,1)S(1)} %get-tuple-element.39.own_ref, bf16[256,1024]{1,0:T(8,128)(2,1)S(1)} %collective-permute-done.10.other_ref), custom_call_target="tpu_custom_call" | custom-call | tf_op jit(solution)/shard_map/pallas_call | solution.py:456
  (2 shorter events, 0.0 us)
Async XLA Ops:
  0.0 2.0 %copy-start = (bf16[2,1,128,256]{3,2,1,0:T(8,128)(2,1)S(1)}, bf16[2,1,128,256]{3,2,1,0:T(8,128)(2,1)}, u32[]{:S(2)}) copy-start(bf16[2,1,128,256]{3,2,1,0:T(8,128)(2,1)} %refs_0_.1) | copy-start | bytes 393220
  0.0 2.0 %copy-start.1 = (bf16[2,1,128,256]{3,2,1,0:T(8,128)(2,1)S(1)}, bf16[2,1,128,256]{3,2,1,0:T(8,128)(2,1)}, u32[]{:S(2)}) copy-start(bf16[2,1,128,256]{3,2,1,0:T(8,128)(2,1)} %refs_1_.1) | copy-start | bytes 393220
  0.0 2.1 %copy-start.3 = (s32[8]{0:T(128)S(1)}, s32[8]{0:T(128)}, u32[]{:S(2)}) copy-start(s32[8]{0:T(128)} %param.8) | copy-start | bytes 100
  0.0 2.5 %copy-start.2 = (s32[8,32]{1,0:T(8,128)S(1)}, s32[8,32]{1,0:T(8,128)}, u32[]{:S(2)}) copy-start(s32[8,32]{1,0:T(8,128)} %param.9) | copy-start | bytes 3076
  0.0 1.9 %collective-permute-start = (bf16[2,1,128,256]{3,2,1,0:T(8,128)(2,1)}, bf16[2,1,128,256]{3,2,1,0:T(8,128)(2,1)S(1)}, u32[]{:S(2)}, u32[]{:S(2)}) collective-permute-start(bf16[2,1,128,256]{3,2,1,0:T(8,128)(2,1)} %refs_0_.1), channel_id=1, source_target_pairs={{0,2},{2,0},{4,6},{6,4},{1,3},{3,1},{5,7},{7,5},{8,10},{10,8},{12,... | collective-permute-start | bytes 393224 | tf_op jit(solution)/shard_map/ppermute | solution.py:43
  0.1 1.9 %collective-permute-start.1 = (bf16[2,1,128,256]{3,2,1,0:T(8,128)(2,1)}, bf16[2,1,128,256]{3,2,1,0:T(8,128)(2,1)S(1)}, u32[]{:S(2)}, u32[]{:S(2)}) collective-permute-start(bf16[2,1,128,256]{3,2,1,0:T(8,128)(2,1)} %refs_1_.1), channel_id=1, source_target_pairs={{0,2},{2,0},{4,6},{6,4},{1,3},{3,1},{5,7},{7,5},{8,10},{10,8},{12,... | collective-permute-start | bytes 393224 | tf_op jit(solution)/shard_map/ppermute | solution.py:43
  2.2 8.5 %collective-permute-start.2 = (bf16[8,128,128]{2,1,0:T(8,128)(2,1)S(1)}, bf16[8,128,128]{2,1,0:T(8,128)(2,1)S(1)}, u32[]{:S(2)}, u32[]{:S(2)}) collective-permute-start(bf16[8,128,128]{2,1,0:T(8,128)(2,1)S(1)} %shard_map.55.refs_0_.refs_2_), channel_id=1, source_target_pairs={{0,16},{16,24},{24,8},{8,0},{1,17},{17,25},{25,9},{9,1},{2,18},{18... | collective-permute-start | bytes 786440 | tf_op jit(solution)/shard_map/ppermute | solution.py:27
  3.6 13.3 %collective-permute-start.3 = (bf16[8,128,128]{2,1,0:T(8,128)(2,1)S(1)}, bf16[8,128,128]{2,1,0:T(8,128)(2,1)S(1)}, u32[]{:S(2)}, u32[]{:S(2)}) collective-permute-start(bf16[8,128,128]{2,1,0:T(8,128)(2,1)S(1)} %shard_map.55.refs_0_.refs_2_), channel_id=1, source_target_pairs={{0,8},{16,0},{24,16},{8,24},{1,9},{17,1},{25,17},{9,25},{2,10},{18... | collective-permute-start | bytes 786440 | tf_op jit(solution)/shard_map/ppermute | solution.py:27
  6.3 11.7 %collective-permute-start.6 = (bf16[8,128,128]{2,1,0:T(8,128)(2,1)S(1)}, bf16[8,128,128]{2,1,0:T(8,128)(2,1)S(1)}, u32[]{:S(2)}, u32[]{:S(2)}) collective-permute-start(bf16[8,128,128]{2,1,0:T(8,128)(2,1)S(1)} %shard_map.55.refs_0_.refs_2_), channel_id=1, source_target_pairs={{0,4},{2,6},{4,0},{6,2},{1,5},{3,7},{5,1},{7,3},{8,12},{10,14},{12... | collective-permute-start | bytes 786440 | tf_op jit(solution)/shard_map/ppermute | solution.py:43
  10.6 9.3 %collective-permute-start.5 = (bf16[8,128,128]{2,1,0:T(8,128)(2,1)S(1)}, bf16[8,128,128]{2,1,0:T(8,128)(2,1)S(1)}, u32[]{:S(2)}, u32[]{:S(2)}) collective-permute-start(bf16[8,128,128]{2,1,0:T(8,128)(2,1)S(1)} %collective-permute-done.2.refs_0_.refs_3_), channel_id=1, source_target_pairs={{0,4},{2,6},{4,0},{6,2},{1,5},{3,7},{5,1},{7,3},{8,12},{10,14},{12... | collective-permute-start | bytes 786440 | tf_op jit(solution)/shard_map/ppermute | solution.py:43
  16.9 8.2 %collective-permute-start.4 = (bf16[8,128,128]{2,1,0:T(8,128)(2,1)S(1)}, bf16[8,128,128]{2,1,0:T(8,128)(2,1)S(1)}, u32[]{:S(2)}, u32[]{:S(2)}) collective-permute-start(bf16[8,128,128]{2,1,0:T(8,128)(2,1)S(1)} %collective-permute-done.2.refs_0_.refs_3_), channel_id=1, source_target_pairs={{0,16},{16,24},{24,8},{8,0},{1,17},{17,25},{25,9},{9,1},{2,18},{18... | collective-permute-start | bytes 786440 | tf_op jit(solution)/shard_map/ppermute | solution.py:27
  17.5 12.6 %collective-permute-start.9 = (bf16[8,128,128]{2,1,0:T(8,128)(2,1)S(1)}, bf16[8,128,128]{2,1,0:T(8,128)(2,1)S(1)}, u32[]{:S(2)}, u32[]{:S(2)}) collective-permute-start(bf16[8,128,128]{2,1,0:T(8,128)(2,1)S(1)} %collective-permute-done.3.refs_0_.refs_4_), channel_id=1, source_target_pairs={{0,4},{2,6},{4,0},{6,2},{1,5},{3,7},{5,1},{7,3},{8,12},{10,14},{12... | collective-permute-start | bytes 786440 | tf_op jit(solution)/shard_map/ppermute | solution.py:43
  25.2 7.3 %collective-permute-start.8 = (bf16[4,128,128]{2,1,0:T(8,128)(2,1)S(1)}, bf16[4,128,128]{2,1,0:T(8,128)(2,1)S(1)}, u32[]{:S(2)}, u32[]{:S(2)}) collective-permute-start(bf16[4,128,128]{2,1,0:T(8,128)(2,1)S(1)} %slice.7), channel_id=1, source_target_pairs={{0,16},{16,24},{24,8},{8,0},{1,17},{17,25},{25,9},{9,1},{2,18},{18... | collective-permute-start | bytes 393224 | tf_op jit(solution)/shard_map/ppermute | solution.py:27
  26.4 6.1 %collective-permute-start.7 = (bf16[4,128,128]{2,1,0:T(8,128)(2,1)S(1)}, bf16[4,128,128]{2,1,0:T(8,128)(2,1)S(1)}, u32[]{:S(2)}, u32[]{:S(2)}) collective-permute-start(bf16[4,128,128]{2,1,0:T(8,128)(2,1)S(1)} %slice.6), channel_id=1, source_target_pairs={{0,4},{2,6},{4,0},{6,2},{1,5},{3,7},{5,1},{7,3},{8,12},{10,14},{12... | collective-permute-start | bytes 393224 | tf_op jit(solution)/shard_map/ppermute | solution.py:43
  34.7 22.2 %collective-permute-start.10 = (bf16[256,1024]{1,0:T(8,128)(2,1)S(1)}, bf16[256,1024]{1,0:T(8,128)(2,1)S(1)}, u32[]{:S(2)}, u32[]{:S(2)}) collective-permute-start(bf16[256,1024]{1,0:T(8,128)(2,1)S(1)} %get-tuple-element.40), channel_id=1, source_target_pairs={{0,2},{2,0},{4,6},{6,4},{1,3},{3,1},{5,7},{7,5},{8,10},{10,8},{12,... | collective-permute-start | bytes 1572872 | tf_op jit(solution)/shard_map/ppermute | solution.py:43
where the time goes:
time: 56.9 us; the launch traced here: 58 us
  Pallas kernels  29.1 us (51%)
  starting transfers between devices  17.4 us (31%)
  waiting for transfers between devices  11.1 us (20%)
    pallas_call x8, Pallas kernels, call(): pl.pallas_call(functools.partial(attend_stage, (pb, ka, cores, class_loca...  26.5 us
    ppermute x7, starting transfers between devices, turn(): return lax.ppermute(array, 'ka', pairs)  12.6 us
    ppermute x4, waiting for transfers between devices, along_ring(): lax.ppermute(array, 'pb', [(ring[i], ring[(i + step) % size]) for i in ra...  11.1 us
    ppermute x4, starting transfers between devices, along_ring(): lax.ppermute(array, 'pb', [(ring[i], ring[(i + step) % size]) for i in ra...  4.84 us
    pallas_call x1, Pallas kernels, on_device(): pl.pallas_call(functools.partial(fetch, cores), out_shape=jax.ShapeDtypeS...  1.35 us
  transfers between devices with their start and end apart: 11, of which 3 were waited for; matrix products, arithmetic and copies ran while one was open for 0% of the time, Pallas kernels for 44%

commit v1 on v0

--- a/solution.py
+++ b/solution.py
@@ -429,8 +429,7 @@
         state = work(state, [on_others], [([1], 1, every)])
         two, state = tie((two, state))
         two_low = turn(two[:half], ka, cores, 1, 0)
-        state = work(state, [two], [([2], 0, every)])
-        state = work(state, [back_others], [([pb - 1], 1, every)])
+        state = work(state, [two, back_others], [([2], 0, every), ([pb - 1], 1, every)])
         pieces, places = [two_low, two_high], [([2], 1, [0]), ([2], 1, [1])]
     else:
         arrived = [start] + along(start, sources - 1)

time: 56.9 us -> 57 us (level)
  the two profiles are of different devices: /device:TPU:28 before, /device:TPU:1 now
where the time goes in v1:
time: 57 us; the launch traced here: 56.3 us
  Pallas kernels  26.3 us (46%)
  starting transfers between devices  22.2 us (39%)
  waiting for transfers between devices  7.33 us (13%)
    pallas_call x7, Pallas kernels, call(): pl.pallas_call(functools.partial(attend_stage, (pb, ka, cores, class_loca...  23.8 us
    ppermute x7, starting transfers between devices, turn(): return lax.ppermute(array, 'ka', pairs)  18 us
    ppermute x4, waiting for transfers between devices, along_ring(): lax.ppermute(array, 'pb', [(ring[i], ring[(i + step) % size]) for i in ra...  6.39 us
    ppermute x4, starting transfers between devices, along_ring(): lax.ppermute(array, 'pb', [(ring[i], ring[(i + step) % size]) for i in ra...  4.2 us
    pallas_call x1, Pallas kernels, on_device(): pl.pallas_call(functools.partial(fetch, cores), out_shape=jax.ShapeDtypeS...  1.35 us
  transfers between devices with their start and end apart: 11, of which 5 were waited for; matrix products, arithmetic and copies ran while one was open for 0% of the time, Pallas kernels for 43%

profile of v1, /device:TPU:1, one launch (start us, length us, event | category | flops | bytes accessed | tf_op | source)
XLA Modules:
  0.0 56.3 jit_solution(9261276932929356759)
XLA Ops:
  0.0 0.0 copy-start
  0.0 0.0 copy-start.1
  0.0 0.0 copy-start.3
  0.0 0.0 copy-start.2
  0.0 0.1 collective-permute-start
  0.1 0.5 collective-permute-start.1
  0.6 1.3 %shard_map.56.q_ref = bf16[512,1024]{1,0:T(8,128)(2,1)S(1)} custom-call(bf16[1024,2048]{1,0:T(8,128)(2,1)} %queries_ref.1), custom_call_target="tpu_custom_call" | custom-call | tf_op jit(solution)/shard_map/pallas_call | solution.py:317
  2.0 0.0 collective-permute-done.refs_2_
  2.0 0.0 collective-permute-done.1.refs_3_
  2.0 0.0 copy-done
  2.0 0.0 copy-done.1
  2.0 0.1 shard_map.55.refs_0_.refs_2_
  2.1 0.0 copy-done.3
  2.1 0.1 copy.12
  2.2 3.4 %collective-permute-start.2 = (bf16[8,128,128]{2,1,0:T(8,128)(2,1)S(1)}, bf16[8,128,128]{2,1,0:T(8,128)(2,1)S(1)}, u32[]{:S(2)}, u32[]{:S(2)}) collective-permute-start(bf16[8,128,128]{2,1,0:T(8,128)(2,1)S(1)} %shard_map.55.refs_0_.refs_2_), channel_id=1, source_target_pairs={{0,16},{16,24},{24,8},{8,0},{1,17},{17,25},{25,9},{9,1},{2,18},{18... | collective-permute-start | bytes 786440 | tf_op jit(solution)/shard_map/ppermute | solution.py:27
  5.6 0.0 copy-done.2
  5.6 0.1 pad_add_fusion.table_ref
  5.7 2.8 %shard_map.57.refs_1_ = f32[4,1024,256]{2,1,0:T(8,128)S(1)} custom-call(s32[8,33]{1,0:T(8,128)S(1)} %pad_add_fusion.table_ref, bf16[512,1024]{1,0:T(8,128)(2,1)S(1)} %shard_map.56.q_ref, bf16[8,128,128]{2,1,0:T(8,128)(2,1)S(1)} %shard_map.55.refs_0_.refs_2_), custom_call_target="tpu_custom_call" | custom-call | flops 2147483648 | bytes 4194304 | tf_op jit(solution)/shard_map/pallas_call | solution.py:365
  8.5 0.1 collective-permute-start.3
  8.6 1.2 %collective-permute-start.6 = (bf16[8,128,128]{2,1,0:T(8,128)(2,1)S(1)}, bf16[8,128,128]{2,1,0:T(8,128)(2,1)S(1)}, u32[]{:S(2)}, u32[]{:S(2)}) collective-permute-start(bf16[8,128,128]{2,1,0:T(8,128)(2,1)S(1)} %shard_map.55.refs_0_.refs_2_), channel_id=1, source_target_pairs={{0,4},{2,6},{4,0},{6,2},{1,5},{3,7},{5,1},{7,3},{8,12},{10,14},{12... | collective-permute-start | bytes 786440 | tf_op jit(solution)/shard_map/ppermute | solution.py:43
  9.8 1.2 %collective-permute-done.2.refs_0_.refs_3_ = bf16[8,128,128]{2,1,0:T(8,128)(2,1)S(1)} collective-permute-done((bf16[8,128,128]{2,1,0:T(8,128)(2,1)S(1)}, bf16[8,128,128]{2,1,0:T(8,128)(2,1)S(1)}, u32[]{:S(2)}, u32[]{:S(2)}) %collective-permute-start.2) | collective-permute-done | bytes 262176 | tf_op jit(solution)/shard_map/ppermute | solution.py:27
  11.0 1.2 %collective-permute-start.5 = (bf16[8,128,128]{2,1,0:T(8,128)(2,1)S(1)}, bf16[8,128,128]{2,1,0:T(8,128)(2,1)S(1)}, u32[]{:S(2)}, u32[]{:S(2)}) collective-permute-start(bf16[8,128,128]{2,1,0:T(8,128)(2,1)S(1)} %collective-permute-done.2.refs_0_.refs_3_), channel_id=1, source_target_pairs={{0,4},{2,6},{4,0},{6,2},{1,5},{3,7},{5,1},{7,3},{8,12},{10,14},{12... | collective-permute-start | bytes 786440 | tf_op jit(solution)/shard_map/ppermute | solution.py:43
  12.2 2.3 %shard_map.58.refs_2_ = f32[4,1024,256]{2,1,0:T(8,128)S(1)} custom-call(s32[8,33]{1,0:T(8,128)S(1)} %pad_add_fusion.table_ref, bf16[512,1024]{1,0:T(8,128)(2,1)S(1)} %shard_map.56.q_ref, bf16[8,128,128]{2,1,0:T(8,128)(2,1)S(1)} %collective-permute-done.2.refs_0_.refs_3_, f32[4,1024,256]{2,1,0:T(8,128)S(1)} %shard_map.57.refs_1_), custom_call_target="tpu_custom_call", output_to_operand_aliasing={{}: (3, {})} | custom-call | flops 2147483648 | bytes 4194304 | tf_op jit(solution)/shard_map/pallas_call | solution.py:365
  14.5 4.4 %collective-permute-done.3.refs_0_.refs_4_ = bf16[8,128,128]{2,1,0:T(8,128)(2,1)S(1)} collective-permute-done((bf16[8,128,128]{2,1,0:T(8,128)(2,1)S(1)}, bf16[8,128,128]{2,1,0:T(8,128)(2,1)S(1)}, u32[]{:S(2)}, u32[]{:S(2)}) %collective-permute-start.3) | collective-permute-done | bytes 262176 | tf_op jit(solution)/shard_map/ppermute | solution.py:27
  18.9 0.0 collective-permute-start.4
  18.9 1.3 %collective-permute-start.9 = (bf16[8,128,128]{2,1,0:T(8,128)(2,1)S(1)}, bf16[8,128,128]{2,1,0:T(8,128)(2,1)S(1)}, u32[]{:S(2)}, u32[]{:S(2)}) collective-permute-start(bf16[8,128,128]{2,1,0:T(8,128)(2,1)S(1)} %collective-permute-done.3.refs_0_.refs_4_), channel_id=1, source_target_pairs={{0,4},{2,6},{4,0},{6,2},{1,5},{3,7},{5,1},{7,3},{8,12},{10,14},{12... | collective-permute-start | bytes 786440 | tf_op jit(solution)/shard_map/ppermute | solution.py:43
  20.2 0.0 collective-permute-done.6.refs_1_.refs_5_
  20.2 2.8 %shard_map.59.refs_1_ = f32[4,1024,256]{2,1,0:T(8,128)S(1)} custom-call(s32[8,33]{1,0:T(8,128)S(1)} %pad_add_fusion.table_ref, bf16[512,1024]{1,0:T(8,128)(2,1)S(1)} %shard_map.56.q_ref, bf16[8,128,128]{2,1,0:T(8,128)(2,1)S(1)} %collective-permute-done.3.refs_0_.refs_4_, ...), custom_call_target="tpu_custom_call", output_to_operand_aliasing={{}: (4, {})} | custom-call | flops 2147483648 | bytes 4194304 | tf_op jit(solution)/shard_map/pallas_call | solution.py:365
  23.0 0.0 collective-permute-done.5.refs_0_.refs_6_
  23.0 2.7 %shard_map.60.refs_2_ = f32[4,1024,256]{2,1,0:T(8,128)S(1)} custom-call(s32[8,33]{1,0:T(8,128)S(1)} %pad_add_fusion.table_ref, bf16[512,1024]{1,0:T(8,128)(2,1)S(1)} %shard_map.56.q_ref, bf16[8,128,128]{2,1,0:T(8,128)(2,1)S(1)} %collective-permute-done.5.refs_0_.refs_6_, f32[4,1024,256]{2,1,0:T(8,128)S(1)} %shard_map.59.refs_1_), custom_call_target="tpu_custom_call", output_to_operand_aliasing={{}: (3, {})} | custom-call | flops 2147483648 | bytes 4194304 | tf_op jit(solution)/shard_map/pallas_call | solution.py:365
  25.7 0.4 collective-permute-done.4.refs_0_.refs_7_
  26.1 0.7 %collective-permute-start.8 = (bf16[4,128,128]{2,1,0:T(8,128)(2,1)S(1)}, bf16[4,128,128]{2,1,0:T(8,128)(2,1)S(1)}, u32[]{:S(2)}, u32[]{:S(2)}) collective-permute-start(bf16[4,128,128]{2,1,0:T(8,128)(2,1)S(1)} %slice.7), channel_id=1, source_target_pairs={{0,16},{16,24},{24,8},{8,0},{1,17},{17,25},{25,9},{9,1},{2,18},{18... | collective-permute-start | bytes 393224 | tf_op jit(solution)/shard_map/ppermute | solution.py:27
  26.8 1.3 %collective-permute-start.7 = (bf16[4,128,128]{2,1,0:T(8,128)(2,1)S(1)}, bf16[4,128,128]{2,1,0:T(8,128)(2,1)S(1)}, u32[]{:S(2)}, u32[]{:S(2)}) collective-permute-start(bf16[4,128,128]{2,1,0:T(8,128)(2,1)S(1)} %slice.6), channel_id=1, source_target_pairs={{0,4},{2,6},{4,0},{6,2},{1,5},{3,7},{5,1},{7,3},{8,12},{10,14},{12... | collective-permute-start | bytes 393224 | tf_op jit(solution)/shard_map/ppermute | solution.py:43
  28.0 0.0 collective-permute-done.9.refs_1_.refs_8_
  28.0 1.5 %shard_map.61.refs_9_ = f32[4,1024,256]{2,1,0:T(8,128)S(1)} custom-call(s32[8,33]{1,0:T(8,128)S(1)} %pad_add_fusion.table_ref, bf16[512,1024]{1,0:T(8,128)(2,1)S(1)} %shard_map.56.q_ref, bf16[8,128,128]{2,1,0:T(8,128)(2,1)S(1)} %collective-permute-done.4.refs_0_.refs_7_, ...), custom_call_target="tpu_custom_call", output_to_operand_aliasing={{}: (4, {})} | custom-call | flops 2147483648 | bytes 4194304 | tf_op jit(solution)/shard_map/pallas_call | solution.py:365
  29.5 0.4 collective-permute-done.8.refs_1_
  30.0 0.9 %collective-permute-done.7.refs_0_ = bf16[4,128,128]{2,1,0:T(8,128)(2,1)S(1)} collective-permute-done((bf16[4,128,128]{2,1,0:T(8,128)(2,1)S(1)}, bf16[4,128,128]{2,1,0:T(8,128)(2,1)S(1)}, u32[]{:S(2)}, u32[]{:S(2)}) %collective-permute-start.7) | collective-permute-done | bytes 131104 | tf_op jit(solution)/shard_map/ppermute | solution.py:43
  30.9 1.2 %shard_map.62 = (f32[4,1024,256]{2,1,0:T(8,128)S(1)}, bf16[256,1024]{1,0:T(8,128)(2,1)S(1)}) custom-call(s32[8,33]{1,0:T(8,128)S(1)} %pad_add_fusion.table_ref, bf16[512,1024]{1,0:T(8,128)(2,1)S(1)} %shard_map.56.q_ref, bf16[4,128,128]{2,1,0:T(8,128)(2,1)S(1)} %collective-permute-done.7.refs_0_, ...), custom_call_target="tpu_custom_call", output_to_operand_aliasing={{0}: (11, {})} | custom-call | flops 2147483648 | bytes 4194304 | tf_op jit(solution)/shard_map/pallas_call | solution.py:365
  32.1 12.5 %collective-permute-start.10 = (bf16[256,1024]{1,0:T(8,128)(2,1)S(1)}, bf16[256,1024]{1,0:T(8,128)(2,1)S(1)}, u32[]{:S(2)}, u32[]{:S(2)}) collective-permute-start(bf16[256,1024]{1,0:T(8,128)(2,1)S(1)} %get-tuple-element.40), channel_id=1, source_target_pairs={{0,2},{2,0},{4,6},{6,4},{1,3},{3,1},{5,7},{7,5},{8,10},{10,8},{12,... | collective-permute-start | bytes 1572872 | tf_op jit(solution)/shard_map/ppermute | solution.py:43
  44.5 10.6 %shard_map.63 = (f32[4,1024,256]{2,1,0:T(8,128)S(1)}, bf16[256,1024]{1,0:T(8,128)(2,1)S(1)}) custom-call(s32[8,33]{1,0:T(8,128)S(1)} %pad_add_fusion.table_ref, bf16[512,1024]{1,0:T(8,128)(2,1)S(1)} %shard_map.56.q_ref, bf16[4,128,128]{2,1,0:T(8,128)(2,1)S(1)} %collective-permute-done.7.refs_0_, ...), custom_call_target="tpu_custom_call", output_to_operand_aliasing={{0}: (11, {})} | custom-call | flops 2147483648 | bytes 4194304 | tf_op jit(solution)/shard_map/pallas_call | solution.py:365
  55.1 0.0 collective-permute-done.10.other_ref
  55.1 1.1 %shard_map.64 = bf16[256,2048]{1,0:T(8,128)(2,1)} custom-call(bf16[256,1024]{1,0:T(8,128)(2,1)S(1)} %get-tuple-element.39.own_ref, bf16[256,1024]{1,0:T(8,128)(2,1)S(1)} %collective-permute-done.10.other_ref), custom_call_target="tpu_custom_call" | custom-call | tf_op jit(solution)/shard_map/pallas_call | solution.py:455
  (2 shorter events, 0.0 us)
Async XLA Ops:
  0.0 2.0 %copy-start = (bf16[2,1,128,256]{3,2,1,0:T(8,128)(2,1)S(1)}, bf16[2,1,128,256]{3,2,1,0:T(8,128)(2,1)}, u32[]{:S(2)}) copy-start(bf16[2,1,128,256]{3,2,1,0:T(8,128)(2,1)} %refs_0_.1) | copy-start | bytes 393220
  0.0 2.0 %copy-start.1 = (bf16[2,1,128,256]{3,2,1,0:T(8,128)(2,1)S(1)}, bf16[2,1,128,256]{3,2,1,0:T(8,128)(2,1)}, u32[]{:S(2)}) copy-start(bf16[2,1,128,256]{3,2,1,0:T(8,128)(2,1)} %refs_1_.1) | copy-start | bytes 393220
  0.0 2.1 %copy-start.3 = (s32[8]{0:T(128)S(1)}, s32[8]{0:T(128)}, u32[]{:S(2)}) copy-start(s32[8]{0:T(128)} %param.8) | copy-start | bytes 100
  0.0 5.6 %copy-start.2 = (s32[8,32]{1,0:T(8,128)S(1)}, s32[8,32]{1,0:T(8,128)}, u32[]{:S(2)}) copy-start(s32[8,32]{1,0:T(8,128)} %param.9) | copy-start | bytes 3076
  0.0 1.9 %collective-permute-start = (bf16[2,1,128,256]{3,2,1,0:T(8,128)(2,1)}, bf16[2,1,128,256]{3,2,1,0:T(8,128)(2,1)S(1)}, u32[]{:S(2)}, u32[]{:S(2)}) collective-permute-start(bf16[2,1,128,256]{3,2,1,0:T(8,128)(2,1)} %refs_0_.1), channel_id=1, source_target_pairs={{0,2},{2,0},{4,6},{6,4},{1,3},{3,1},{5,7},{7,5},{8,10},{10,8},{12,... | collective-permute-start | bytes 393224 | tf_op jit(solution)/shard_map/ppermute | solution.py:43
  0.1 1.8 %collective-permute-start.1 = (bf16[2,1,128,256]{3,2,1,0:T(8,128)(2,1)}, bf16[2,1,128,256]{3,2,1,0:T(8,128)(2,1)S(1)}, u32[]{:S(2)}, u32[]{:S(2)}) collective-permute-start(bf16[2,1,128,256]{3,2,1,0:T(8,128)(2,1)} %refs_1_.1), channel_id=1, source_target_pairs={{0,2},{2,0},{4,6},{6,4},{1,3},{3,1},{5,7},{7,5},{8,10},{10,8},{12,... | collective-permute-start | bytes 393224 | tf_op jit(solution)/shard_map/ppermute | solution.py:43
  2.2 8.8 %collective-permute-start.2 = (bf16[8,128,128]{2,1,0:T(8,128)(2,1)S(1)}, bf16[8,128,128]{2,1,0:T(8,128)(2,1)S(1)}, u32[]{:S(2)}, u32[]{:S(2)}) collective-permute-start(bf16[8,128,128]{2,1,0:T(8,128)(2,1)S(1)} %shard_map.55.refs_0_.refs_2_), channel_id=1, source_target_pairs={{0,16},{16,24},{24,8},{8,0},{1,17},{17,25},{25,9},{9,1},{2,18},{18... | collective-permute-start | bytes 786440 | tf_op jit(solution)/shard_map/ppermute | solution.py:27
  8.5 10.4 %collective-permute-start.3 = (bf16[8,128,128]{2,1,0:T(8,128)(2,1)S(1)}, bf16[8,128,128]{2,1,0:T(8,128)(2,1)S(1)}, u32[]{:S(2)}, u32[]{:S(2)}) collective-permute-start(bf16[8,128,128]{2,1,0:T(8,128)(2,1)S(1)} %shard_map.55.refs_0_.refs_2_), channel_id=1, source_target_pairs={{0,8},{16,0},{24,16},{8,24},{1,9},{17,1},{25,17},{9,25},{2,10},{18... | collective-permute-start | bytes 786440 | tf_op jit(solution)/shard_map/ppermute | solution.py:27
  8.6 11.6 %collective-permute-start.6 = (bf16[8,128,128]{2,1,0:T(8,128)(2,1)S(1)}, bf16[8,128,128]{2,1,0:T(8,128)(2,1)S(1)}, u32[]{:S(2)}, u32[]{:S(2)}) collective-permute-start(bf16[8,128,128]{2,1,0:T(8,128)(2,1)S(1)} %shard_map.55.refs_0_.refs_2_), channel_id=1, source_target_pairs={{0,4},{2,6},{4,0},{6,2},{1,5},{3,7},{5,1},{7,3},{8,12},{10,14},{12... | collective-permute-start | bytes 786440 | tf_op jit(solution)/shard_map/ppermute | solution.py:43
  11.0 12.0 %collective-permute-start.5 = (bf16[8,128,128]{2,1,0:T(8,128)(2,1)S(1)}, bf16[8,128,128]{2,1,0:T(8,128)(2,1)S(1)}, u32[]{:S(2)}, u32[]{:S(2)}) collective-permute-start(bf16[8,128,128]{2,1,0:T(8,128)(2,1)S(1)} %collective-permute-done.2.refs_0_.refs_3_), channel_id=1, source_target_pairs={{0,4},{2,6},{4,0},{6,2},{1,5},{3,7},{5,1},{7,3},{8,12},{10,14},{12... | collective-permute-start | bytes 786440 | tf_op jit(solution)/shard_map/ppermute | solution.py:43
  18.9 7.2 %collective-permute-start.4 = (bf16[8,128,128]{2,1,0:T(8,128)(2,1)S(1)}, bf16[8,128,128]{2,1,0:T(8,128)(2,1)S(1)}, u32[]{:S(2)}, u32[]{:S(2)}) collective-permute-start(bf16[8,128,128]{2,1,0:T(8,128)(2,1)S(1)} %collective-permute-done.2.refs_0_.refs_3_), channel_id=1, source_target_pairs={{0,16},{16,24},{24,8},{8,0},{1,17},{17,25},{25,9},{9,1},{2,18},{18... | collective-permute-start | bytes 786440 | tf_op jit(solution)/shard_map/ppermute | solution.py:27
  18.9 9.2 %collective-permute-start.9 = (bf16[8,128,128]{2,1,0:T(8,128)(2,1)S(1)}, bf16[8,128,128]{2,1,0:T(8,128)(2,1)S(1)}, u32[]{:S(2)}, u32[]{:S(2)}) collective-permute-start(bf16[8,128,128]{2,1,0:T(8,128)(2,1)S(1)} %collective-permute-done.3.refs_0_.refs_4_), channel_id=1, source_target_pairs={{0,4},{2,6},{4,0},{6,2},{1,5},{3,7},{5,1},{7,3},{8,12},{10,14},{12... | collective-permute-start | bytes 786440 | tf_op jit(solution)/shard_map/ppermute | solution.py:43
  26.1 3.9 %collective-permute-start.8 = (bf16[4,128,128]{2,1,0:T(8,128)(2,1)S(1)}, bf16[4,128,128]{2,1,0:T(8,128)(2,1)S(1)}, u32[]{:S(2)}, u32[]{:S(2)}) collective-permute-start(bf16[4,128,128]{2,1,0:T(8,128)(2,1)S(1)} %slice.7), channel_id=1, source_target_pairs={{0,16},{16,24},{24,8},{8,0},{1,17},{17,25},{25,9},{9,1},{2,18},{18... | collective-permute-start | bytes 393224 | tf_op jit(solution)/shard_map/ppermute | solution.py:27
  26.8 4.1 %collective-permute-start.7 = (bf16[4,128,128]{2,1,0:T(8,128)(2,1)S(1)}, bf16[4,128,128]{2,1,0:T(8,128)(2,1)S(1)}, u32[]{:S(2)}, u32[]{:S(2)}) collective-permute-start(bf16[4,128,128]{2,1,0:T(8,128)(2,1)S(1)} %slice.6), channel_id=1, source_target_pairs={{0,4},{2,6},{4,0},{6,2},{1,5},{3,7},{5,1},{7,3},{8,12},{10,14},{12... | collective-permute-start | bytes 393224 | tf_op jit(solution)/shard_map/ppermute | solution.py:43
  32.1 23.1 %collective-permute-start.10 = (bf16[256,1024]{1,0:T(8,128)(2,1)S(1)}, bf16[256,1024]{1,0:T(8,128)(2,1)S(1)}, u32[]{:S(2)}, u32[]{:S(2)}) collective-permute-start(bf16[256,1024]{1,0:T(8,128)(2,1)S(1)} %get-tuple-element.40), channel_id=1, source_target_pairs={{0,2},{2,0},{4,6},{6,4},{1,3},{3,1},{5,7},{7,5},{8,10},{10,8},{12,... | collective-permute-start | bytes 1572872 | tf_op jit(solution)/shard_map/ppermute | solution.py:43
